TPU v7x, 128 devices: a whole 4x4x4 slice. The times are simulated.
128 devices in a mesh: group: 16 (over x, y_lo, core), tensor: 8 (over y_hi, z).
Axes of the slice: x: 4, y: 4 (y_hi: 2, y_lo: 2; y = y_hi * 2 + y_lo), z: 4, core: 2. Of those that a mesh axis runs over, the one named last changes fastest.
Arguments:
- tokens: bfloat16 [2, 64, 8192], P(None, 'group'), may hold values from -6 to 6
- queries: bfloat16 [2, 2, 64, 8192], P(None, None, 'group', 'tensor'), may hold values from -40 to 40
- cache_kv: bfloat16 [2, 64, 2048, 2048], P(None, 'group', None, 'tensor'), may hold values from -40 to 40
- old_kv: bfloat16 [2, 8192, 2048], P(None, None, 'tensor'), may hold values from -0.0625 to 0.0625
- new_kv: bfloat16 [2, 8192, 2048], P(None, 'group', 'tensor'), may hold values from -0.0625 to 0.0625
- switch: int32 [2], replicated, may hold values from 0 to 1, each once
- lengths: int32 [64], P('group'), may hold values from 1 to 2048, as said below
Outputs:
- hidden_out: bfloat16 [2, 64, 8192], P(None, 'group', 'tensor')
Inputs may be any that keep to these rules, and one draw needn't show every extreme that they name: `switch`: the entries are a permutation of 0 to 1; a layer uses new_kv at every step from its entry on. `lengths`: sequences with an odd index hold 1 to 8 valid positions, sequence 1 exactly 1 and sequence 3 exactly 8; sequences with an even index hold 512 to 2048, sequence 0 exactly 2048.
All inputs are finite; a program needn't handle non-finite values.
Results may differ from a plain program's by a relative error of at most 0.0075.
Values may be sent and summed in bfloat16 or wider, within the bound.
A program may use at most 128 MiB of HBM per device.

v0:
```python
import jax
import jax.numpy as jnp
from jax import lax
from jax.sharding import PartitionSpec as P

QPK = 8
HD = 128
LAYERS = 2


def normalize(values):
    return values * lax.rsqrt(jnp.mean(values * values, axis=-1, keepdims=True) + 1e-05)


def attend_local(query_heads, cache_here, fresh, lengths):
    steps_n = query_heads.shape[0]
    cache_len = cache_here.shape[1]
    scale = HD ** (-0.5)
    score_old = (
        jnp.einsum(
            "tsjid,scjd->tsjic",
            query_heads,
            cache_here[:, :, :, 0],
            preferred_element_type=jnp.float32,
        )
        * scale
    )
    valid = jnp.arange(cache_len)[None, :] < lengths[:, None]
    score_old = jnp.where(valid[None, :, None, None, :], score_old, -1e30)
    score_new = (
        jnp.einsum(
            "tsjid,usjd->tsjiu", query_heads, fresh[:, :, :, 0], preferred_element_type=jnp.float32
        )
        * scale
    )
    causal = jnp.arange(steps_n)[None, :] <= jnp.arange(steps_n)[:, None]
    score_new = jnp.where(causal[:, None, None, None, :], score_new, -1e30)
    top = jnp.maximum(score_old.max(-1, keepdims=True), score_new.max(-1, keepdims=True))
    exp_old = jnp.exp(score_old - top)
    exp_new = jnp.exp(score_new - top)
    total = exp_old.sum(-1, keepdims=True) + exp_new.sum(-1, keepdims=True)
    weight_old = (exp_old / total).astype(jnp.bfloat16)
    weight_new = (exp_new / total).astype(jnp.bfloat16)
    mixed = jnp.einsum(
        "tsjic,scjd->tsjid", weight_old, cache_here[:, :, :, 1], preferred_element_type=jnp.float32
    )
    mixed = mixed + jnp.einsum(
        "tsjiu,usjd->tsjid", weight_new, fresh[:, :, :, 1], preferred_element_type=jnp.float32
    )
    return mixed.astype(jnp.bfloat16)


def per_device(tokens, queries, cache_kv, old_kv, new_kv, switch, lengths):
    steps_n, seqs, width = tokens.shape
    columns = old_kv.shape[2]
    heads_dev = columns // (2 * HD)
    cache_len = cache_kv.shape[2]
    rows = steps_n * seqs
    step_ids = jnp.arange(steps_n)
    hidden = tokens.astype(jnp.float32)
    result = tokens
    for layer in range(LAYERS):
        normed = normalize(hidden).astype(jnp.bfloat16)
        flat_rows = normed.reshape(rows, width)
        old_proj = jnp.dot(flat_rows, old_kv[layer], preferred_element_type=jnp.float32)
        new_shard = new_kv[layer]
        new_proj = jnp.dot(
            flat_rows,
            lax.all_gather(new_shard, "group", axis=0, tiled=True),
            preferred_element_type=jnp.float32,
        )
        use_new = (step_ids >= switch[layer])[:, None, None]
        fresh = jnp.where(
            use_new,
            new_proj.reshape(steps_n, seqs, columns),
            old_proj.reshape(steps_n, seqs, columns),
        )
        fresh = fresh.astype(jnp.bfloat16).reshape(steps_n, seqs, heads_dev, 2, HD)
        query_heads = queries[:, layer].reshape(steps_n, seqs, heads_dev, QPK, HD)
        cache_here = cache_kv[layer].reshape(seqs, cache_len, heads_dev, 2, HD)
        attended = attend_local(query_heads, cache_here, fresh, lengths).reshape(
            steps_n, seqs, heads_dev * QPK * HD
        )
        if layer + 1 < LAYERS:
            gathered = lax.all_gather(attended, "tensor", axis=2, tiled=True)
            hidden = hidden + gathered.astype(jnp.float32)
        else:
            block = width // lax.axis_size("tensor")
            own_columns = lax.dynamic_slice_in_dim(
                hidden, lax.axis_index("tensor") * block, block, 2
            )
            result = (own_columns + attended.astype(jnp.float32)).astype(jnp.bfloat16)
    return result


def solution(mesh):
    return jax.shard_map(
        per_device,
        mesh=mesh,
        in_specs=(
            P(None, "group", None),
            P(None, None, "group", "tensor"),
            P(None, "group", None, "tensor"),
            P(None, None, "tensor"),
            P(None, "group", "tensor"),
            P(),
            P("group"),
        ),
        out_specs=P(None, "group", "tensor"),
        check_vma=False,
    )
```

profile of v0, /device:TPU:0, one launch (start us, length us, event | category | flops | bytes accessed | tf_op | source)
XLA Modules:
  0.0 106.5 jit_solution(15430903331954702275)
XLA Ops:
  6.5 1.9 %fusion.62 = (bf16[1,512,256]{2,1,0:T(8,128)(2,1)}, bf16[1,512,256]{2,1,0:T(8,128)(2,1)}) fusion(bf16[2,512,256]{2,1,0:T(8,128)(2,1)} %param.11), kind=kLoop, calls=%fused_computation.88 | loop fusion | bytes 1048576 | tf_op jit(solution)/shard_map/slice | solution.py:66
  8.5 0.7 all-gather.7.cloned.1.call-update
  9.2 0.8 fusion.63
  10.0 5.7 %fusion.61 = (bf16[1,4,2048,256]{3,2,1,0:T(8,128)(2,1)}, bf16[1,4,2048,256]{3,2,1,0:T(8,128)(2,1)}) fusion(bf16[2,4,2048,256]{3,2,1,0:T(8,128)(2,1)} %param.9), kind=kLoop, calls=%fused_computation.87 | loop fusion | bytes 16777216 | tf_op jit(solution)/shard_map/slice | solution.py:80
  15.7 6.3 %copy.56 = bf16[1,4,2048,256]{2,3,1,0:T(8,128)(2,1)} copy(bf16[1,4,2048,256]{3,2,1,0:T(8,128)(2,1)} %get-tuple-element.5) | data formatting | bytes 8388608
  22.0 6.4 %copy.61 = bf16[1,4,2048,256]{2,3,1,0:T(8,128)(2,1)} copy(bf16[1,4,2048,256]{3,2,1,0:T(8,128)(2,1)} %get-tuple-element.6) | data formatting | bytes 8388608
  28.4 0.6 fusion.66
  28.9 0.6 iota_compare_fusion.3
  29.5 0.7 iota_compare_fusion.2
  30.2 0.2 fusion.40
  30.5 2.1 %fusion.67 = (f32[2,4,8]{2,0,1:T(2,128)S(1)}, f32[2,4,1,8,2048]{4,3,0,1,2:T(8,128)S(1)}) fusion(bf16[2,4,8,128]{3,2,1,0:T(8,128)(2,1)S(1)} %reshape.262, bf16[4,2048,1,2,128]{1,4,3,0,2:T(8,128)(2,1)} %bitcast.169, pred[4,2048]{1,0:T(4,128)(4,1)S(1)} %iota_compare_fusion), kind=kOutput, calls=%fused_computation.93 | convolution fusion | flops 33947584 | bytes 2646272 | tf_op jit(solution)/shard_map/tsjid,scjd->tsjic/dot_general | solution.py:20
  32.5 2.1 %fusion.68 = (f32[2,4,8]{2,0,1:T(2,128)S(1)}, f32[2,4,1,8,2048]{4,3,0,1,2:T(8,128)S(1)}) fusion(bf16[2,4,8,128]{3,2,1,0:T(8,128)(2,1)S(1)} %reshape.263, bf16[4,2048,1,2,128]{1,4,3,0,2:T(8,128)(2,1)} %bitcast.167, pred[4,2048]{1,0:T(4,128)(4,1)S(1)} %iota_compare_fusion), kind=kOutput, calls=%fused_computation.94 | convolution fusion | flops 33947584 | bytes 2646272 | tf_op jit(solution)/shard_map/tsjid,scjd->tsjic/dot_general | solution.py:20
  34.7 3.0 %fusion.4 = bf16[2,4,256]{2,1,0:T(4,128)(2,1)S(1)} fusion(bf16[2,8192,256]{2,1,0:T(8,128)(2,1)} %param.10, bf16[2,4,8192]{2,1,0:T(4,128)(2,1)S(1)} %copy-done, f32[2,4]{1,0:T(2,128)S(1)} %add_rsqrt_fusion.1), kind=kOutput, calls=%fused_computation.4 | convolution fusion | flops 33751040 | bytes 4329504 | tf_op jit(solution)/shard_map/dot_general | solution.py:65
  37.6 11.3 %all-gather.5.cloned.1.call-done = bf16[1,8192,256]{2,1,0:T(8,128)(2,1)} async-done(((bf16[1,512,256]{2,1,0:T(8,128)(2,1)}), bf16[1,8192,256]{2,1,0:T(8,128)(2,1)}) %all-gather.5.cloned.1.call-update) | async-done | bytes 4194320 | tf_op jit(solution)/shard_map/all_gather | solution.py:69
  48.9 2.9 %fusion.35 = bf16[2,4,256]{2,1,0:T(4,128)(2,1)S(1)} fusion(bf16[2,4,256]{2,1,0:T(4,128)(2,1)S(1)} %fusion.4, bf16[1,8192,256]{2,1,0:T(8,128)(2,1)} %all-gather.5.cloned.1.call-done, bf16[2,4,8192]{2,1,0:T(4,128)(2,1)S(1)} %copy-done, f32[2,4]{1,0:T(2,128)S(1)} %add_rsqrt_fusion.1, pred[2]{0:T(512)(128)(4,1)S(1)} %iota_compare_fusion.3), kind=kOutput, calls=%fused_computation.39 | convolution fusion | flops 33753088 | bytes 4333602 | tf_op jit(solution)/shard_map/dot_general | solution.py:67
  51.9 0.2 convolution_multiply_fusion.3
  52.0 0.1 fusion.59
  52.1 0.1 fusion.53
  52.2 0.2 fusion.38
  52.6 2.3 %fusion.18 = f32[4,128,2,8]{1,3,2,0:T(8,128)S(1)} fusion(bf16[4,2048,1,2,128]{1,4,3,0,2:T(8,128)(2,1)} %bitcast.170, f32[2,4,1,8,2048]{4,3,0,1,2:T(8,128)S(1)} %get-tuple-element.20, f32[2,4,8]{2,0,1:T(2,128)S(1)} %add.52, f32[2,4,8]{2,0,1:T(2,128)S(1)} %max.16), kind=kOutput, calls=%fused_computation.26 | convolution fusion | flops 33947648 | bytes 2654720 | tf_op jit(solution)/shard_map/tsjic,scjd->tsjid/dot_general | solution.py:44
  54.9 0.2 fusion.25
  55.1 34.5 %all_gather.10 = bf16[2,4,8192]{2,1,0:T(4,128)(2,1)S(1)} all-gather(bf16[2,4,1024]{2,1,0:T(4,128)(2,1)S(1)} %copy.31), channel_id=1, replica_groups=mesh['group'=16,'tensor'=8] {'tensor'}, dimensions={2}, use_global_device_ids=true | all-gather | bytes 147456 | tf_op jit(solution)/shard_map/all_gather | solution.py:85
  89.6 0.2 convert_add_fusion
  89.8 3.0 %fusion = bf16[2,4,256]{2,1,0:T(4,128)(2,1)S(1)} fusion(bf16[2,8192,256]{2,1,0:T(8,128)(2,1)} %param.10, f32[2,4]{1,0:T(2,128)S(1)} %add_rsqrt_fusion, bf16[2,4,8192]{2,1,0:T(4,128)(2,1)S(1)} %copy-done, bf16[2,4,8192]{2,1,0:T(4,128)(2,1)S(1)} %all_gather.10), kind=kOutput, calls=%fused_computation | convolution fusion | flops 33882112 | bytes 4460576 | tf_op jit(solution)/shard_map/dot_general | solution.py:65
  92.8 3.0 %fusion.32 = bf16[2,4,256]{2,1,0:T(4,128)(2,1)S(1)} fusion(bf16[2,4,256]{2,1,0:T(4,128)(2,1)S(1)} %fusion, bf16[1,8192,256]{2,1,0:T(8,128)(2,1)} %all-gather.7.cloned.1.call-done, f32[2,4]{1,0:T(2,128)S(1)} %add_rsqrt_fusion, pred[2]{0:T(512)(128)(4,1)S(1)} %iota_compare_fusion.2, bf16[2,4,8192]{2,1,0:T(4,128)(2,1)S(1)} %copy-done, ...), kind=kOutput, calls=%fused_computation.38 | convolution fusion | flops 33884160 | bytes 4464674 | tf_op jit(solution)/shard_map/dot_general | solution.py:67
  95.8 0.2 convolution_multiply_fusion.2
  96.0 0.1 fusion.60
  96.1 0.1 fusion.54
  96.2 0.2 fusion.39
  96.5 2.3 %fusion.19 = f32[4,128,2,8]{1,3,2,0:T(8,128)S(1)} fusion(bf16[4,2048,1,2,128]{1,4,3,0,2:T(8,128)(2,1)} %bitcast.168, f32[2,4,1,8,2048]{4,3,0,1,2:T(8,128)S(1)} %get-tuple-element.22, f32[2,4,8]{2,0,1:T(2,128)S(1)} %add.57, f32[2,4,8]{2,0,1:T(2,128)S(1)} %max.17), kind=kOutput, calls=%fused_computation.27 | convolution fusion | flops 33947648 | bytes 2654720 | tf_op jit(solution)/shard_map/tsjic,scjd->tsjid/dot_general | solution.py:44
  98.8 0.2 fusion.24
  99.0 0.6 fusion.48
  (29 shorter events, 0.5 us)
Async XLA Ops:
  6.5 42.4 %all-gather.5.cloned.1.call-start = ((), (), s32[]{:S(2)}) async-start(), calls=%async_computation | async-start | bytes 4456448 | tf_op jit(solution)/shard_map/all_gather | solution.py:69
  8.4 84.4 %all-gather.7.cloned.1.call-start = ((), (), s32[]{:S(2)}) async-start(), calls=%async_computation.1 | async-start | bytes 4456448 | tf_op jit(solution)/shard_map/all_gather | solution.py:69
  21.9 6.4 %copy-start.1 = (s32[2]{0:T(128)S(1)}, s32[2]{0:T(128)}, u32[]{:S(2)}) copy-start(s32[2]{0:T(128)} %param.12) | copy-start | bytes 28
  22.0 8.2 %copy-start = (bf16[2,4,8192]{2,1,0:T(4,128)(2,1)S(1)}, bf16[2,4,8192]{2,1,0:T(4,128)(2,1)}, u32[]{:S(2)}) copy-start(bf16[2,4,8192]{2,1,0:T(4,128)(2,1)} %param.7) | copy-start | bytes 393220
  22.0 8.4 %copy-start.2 = (s32[4]{0:T(128)S(1)}, s32[4]{0:T(128)}, u32[]{:S(2)}) copy-start(s32[4]{0:T(128)} %param.13) | copy-start | bytes 52
Sparse Core Ops, SparseCore 0:
  9.1 39.7 all-gather.4
  50.6 37.5 all-gather.6
where the time goes:
time: 107 us; the launch traced here: 106 us
  blocking collectives  34.5 us (32%)
  local copies, waits for them, and re-layouts  21.7 us (20%)
  matrix products  21.3 us (20%)
  between operations  13.6 us (13%)
  waiting for transfers between devices  12 us (11%)
  other arithmetic  3.38 us (3%)
    all_gather x1, blocking collectives, per_device(): gathered = lax.all_gather(attended, 'tensor', axis=2, tiled=True)  34.5 us
    unnamed x8, local copies, waits for them, and re-layouts  12.6 us
    all_gather x2, waiting for transfers between devices, per_device(): lax.all_gather(new_shard, 'group', axis=0, tiled=True)  11.3 us
    dot_general x2, matrix products, per_device(): jnp.dot(flat_rows, old_kv[layer], preferred_element_type=jnp.float32)  5.92 us
    dot_general x2, matrix products, per_device(): jnp.dot(flat_rows, lax.all_gather(new_shard, 'group', axis=0, tiled=True)...  5.88 us
    slice x1, local copies, waits for them, and re-layouts, per_device(): cache_here = cache_kv[layer].reshape(seqs, cache_len, heads_dev, 2, HD)  5.72 us
    dot_general x2, matrix products, attend_local(): jnp.einsum('tsjic,scjd->tsjid', weight_old, cache_here[:, :, :, 1], prefe...  4.58 us
    dot_general x2, matrix products, attend_local(): jnp.einsum('tsjid,scjd->tsjic', query_heads, cache_here[:, :, :, 0], pref...  4.19 us
  transfers between devices with their start and end apart: 2, of which 1 were waited for; matrix products, arithmetic and copies ran while one was open for 35% of the time, Pallas kernels for 0%

commit v1 on v0

v1 whole, which is shorter than its diff:
```python
import functools
import math

import jax
import jax.numpy as jnp
from jax import lax
from jax.experimental import pallas as pl
from jax.experimental.pallas import tpu as pltpu
from jax.sharding import PartitionSpec as P

MESH = pl.DeviceIdType.MESH
F32, BF16 = jnp.float32, jnp.bfloat16
HD = 128
QPK = 8
LAYERS = 2
STEPS = 2
SEQS = 4
ROWS = STEPS * SEQS
SHORT = 16
FAR = -1e30
UNIT = HD**-0.5 * math.log2(math.e)


def stack_rows(ref_value):
    wide = ref_value.astype(F32)
    return jnp.concatenate([wide[0], wide[1]], axis=0)


def kernel(
    groups,
    tensors,
    tokens,
    queries,
    cache,
    old_kv,
    new_kv,
    switch_hbm,
    lengths_hbm,
    out,
    switch,
    lengths,
    tok_v,
    own_v,
    q_v,
    long_v,
    short_v,
    old_v,
    new_v,
    send_a,
    recv_a,
    send_b,
    recv_b,
    send_c,
    recv_c,
    send_d,
    recv_d,
    load_sem,
    long_sem,
    short_sem,
    send_sem,
    recv_sem,
):
    g = lax.axis_index("group")
    t = lax.axis_index("tensor")
    depth = new_kv.shape[1]
    half = depth // 2
    width = tokens.shape[2]
    block = width // tensors
    home = g // 2

    barrier = pltpu.get_barrier_semaphore()
    for k in range(1, groups):
        pl.semaphore_signal(
            barrier,
            inc=1,
            device_id={"group": lax.rem(g + k, groups), "tensor": t},
            device_id_type=MESH,
        )
    for k in range(1, groups):
        pl.semaphore_signal(
            barrier,
            inc=1,
            device_id={"group": lax.rem(g + k, groups), "tensor": home},
            device_id_type=MESH,
        )

    @pl.when(home != t)
    def _():
        pl.semaphore_signal(
            barrier, inc=1, device_id={"group": g, "tensor": home}, device_id_type=MESH
        )

    loads = [
        pltpu.make_async_copy(tokens, tok_v, load_sem.at[0]),
        pltpu.make_async_copy(
            tokens.at[:, :, pl.ds(pl.multiple_of(t * block, block), block)],
            own_v,
            load_sem.at[1],
        ),
        pltpu.make_async_copy(queries, q_v, load_sem.at[2]),
        pltpu.make_async_copy(new_kv, new_v, load_sem.at[3]),
        pltpu.make_async_copy(
            old_kv.at[:, pl.ds(pl.multiple_of(g * depth, depth), depth), :],
            old_v,
            load_sem.at[4],
        ),
        pltpu.make_async_copy(switch_hbm, switch, load_sem.at[5]),
        pltpu.make_async_copy(lengths_hbm, lengths, load_sem.at[6]),
    ]
    longs = [
        [
            pltpu.make_async_copy(
                cache.at[layer, 2 * j], long_v.at[layer, j], long_sem.at[layer, j]
            )
            for j in range(2)
        ]
        for layer in range(LAYERS)
    ]
    shorts = [
        [
            pltpu.make_async_copy(
                cache.at[layer, 2 * j + 1, pl.ds(0, SHORT)],
                short_v.at[layer, j],
                short_sem.at[layer, j],
            )
            for j in range(2)
        ]
        for layer in range(LAYERS)
    ]
    for copy in loads:
        copy.start()
    for layer in range(LAYERS):
        for j in range(2):
            longs[layer][j].start()
            shorts[layer][j].start()

    loads[0].wait()
    mine = stack_rows(tok_v[...])
    for k in range(groups):
        piece = mine[:, k * depth : (k + 1) * depth]
        send_a[k] = jnp.concatenate([piece[:, :half], piece[:, half:]], axis=0).astype(BF16)
    scale_0 = lax.rsqrt(jnp.sum(mine * mine, axis=1, keepdims=True) / width + 1e-05)

    @pl.when(home != t)
    def _():
        pl.semaphore_wait(barrier, 2 * groups - 1)

    @pl.when(home == t)
    def _():
        pl.semaphore_wait(barrier, 2 * groups - 2)

    def whole(ref, sem):
        return pltpu.make_async_copy(ref, ref, sem)

    def to_group(src, dst, phase, sign, by_slot):
        for k in range(1, groups):
            peer = lax.rem(g + (groups + sign * k), groups)
            pltpu.make_async_remote_copy(
                src_ref=src.at[k if by_slot else peer],
                dst_ref=dst.at[k],
                send_sem=send_sem.at[phase],
                recv_sem=recv_sem.at[phase],
                device_id={"group": peer, "tensor": t},
                device_id_type=MESH,
            ).start()

    to_group(send_a, recv_a, 0, 1, False)
    recv_a[0] = send_a[g]

    row = lax.broadcasted_iota(jnp.int32, (QPK * ROWS, 1), 0)
    row_seq = lax.rem(row, SEQS)

    def stale(layer):
        every = stack_rows(q_v[:, layer])
        q = jnp.concatenate([every[:, i * HD : (i + 1) * HD] for i in range(QPK)], axis=0)
        q16 = q.astype(BF16)
        scores = []
        blocks = []
        for j in range(2):
            longs[layer][j].wait()
            shorts[layer][j].wait()
            for held, seq in ((long_v, 2 * j), (short_v, 2 * j + 1)):
                s = lax.dot_general(
                    q16, held[layer, j, :, :HD], (((1,), (1,)), ((), ())), preferred_element_type=F32
                )
                col = lax.broadcasted_iota(jnp.int32, s.shape, 1)
                keep = (col < lengths[seq]) & (row_seq == seq)
                scores.append(jnp.where(keep, s * UNIT, FAR))
                blocks.append((held, j))
        top = functools.reduce(
            jnp.maximum, [jnp.max(s, axis=1, keepdims=True) for s in scores]
        )
        total = jnp.zeros_like(top)
        mixed = jnp.zeros((QPK * ROWS, HD), F32)
        for s, (held, j) in zip(scores, blocks):
            weight = jnp.exp2(s - top)
            total = total + jnp.sum(weight, axis=1, keepdims=True)
            mixed = mixed + jnp.dot(weight.astype(BF16), held[layer, j, :, HD:], preferred_element_type=F32)
        shape = (QPK, ROWS)
        return (
            q.reshape(*shape, HD),
            top.reshape(*shape, 1),
            total.reshape(*shape, 1),
            mixed.reshape(*shape, HD),
        )

    upper = lax.broadcasted_iota(jnp.int32, (ROWS, HD), 0) < SEQS

    def by_step(fresh):
        other = jnp.concatenate([fresh[SEQS:], fresh[:SEQS]], axis=0)
        return jnp.where(upper, fresh, other), jnp.where(upper, other, fresh)

    def merge(fresh, part):
        q, top, total, mixed = part
        fresh = fresh.astype(BF16).astype(F32)
        key_0, key_1 = by_step(fresh[:, :HD])
        value_0, value_1 = by_step(fresh[:, HD:])
        s_0 = jnp.sum(q * key_0[None], axis=2, keepdims=True) * UNIT
        s_1 = jnp.sum(q * key_1[None], axis=2, keepdims=True) * UNIT
        s_1 = jnp.where(upper[None, :, :1], FAR, s_1)
        peak = jnp.maximum(top, jnp.maximum(s_0, s_1))
        keep = jnp.exp2(top - peak)
        w_0 = jnp.exp2(s_0 - peak)
        w_1 = jnp.exp2(s_1 - peak)
        norm = 1.0 / (total * keep + w_0 + w_1)
        result = (mixed * keep + w_0 * value_0[None] + w_1 * value_1[None]) * norm
        return result.astype(BF16).astype(F32)

    def project(layer, features):
        flat = jnp.concatenate(
            [features[:, :ROWS].reshape(-1, half), features[:, ROWS:].reshape(-1, half)], axis=1
        ).astype(BF16)
        by_new = jnp.dot(flat, new_v[layer], preferred_element_type=F32)
        by_old = jnp.dot(flat, old_v[layer], preferred_element_type=F32)
        step = lax.rem(lax.broadcasted_iota(jnp.int32, by_new.shape, 0), ROWS) // SEQS
        picked = jnp.where(step >= switch[layer], by_new, by_old)
        return picked.reshape(groups, ROWS, -1)

    for copy in loads[1:]:
        copy.wait()
    part_0 = stale(0)

    rest = pl.ds(1, groups - 1)
    whole(recv_a.at[rest], recv_sem.at[0]).wait()
    products = project(0, recv_a[...].astype(F32))
    send_b[...] = products
    to_group(send_b, recv_b, 1, -1, True)
    recv_b[0] = products[0]
    part_1 = stale(1)

    whole(recv_b.at[rest], recv_sem.at[1]).wait()
    attended_0 = merge(jnp.sum(recv_b[...], axis=0) * scale_0, part_0)
    pair = QPK // 4
    for h in range(2):
        send_c[h] = jnp.concatenate(
            [
                jnp.concatenate([attended_0[4 * h + 2 * r + c] for c in range(pair)], axis=1)
                for r in range(2)
            ],
            axis=0,
        ).astype(BF16)

    for h in range(2):
        target = 2 * t + h
        slot = lax.rem(target + groups - g, groups)

        def copy_c(j):
            return pltpu.make_async_remote_copy(
                src_ref=send_c.at[h],
                dst_ref=recv_c.at[slot],
                send_sem=send_sem.at[2],
                recv_sem=recv_sem.at[2],
                device_id={"group": target, "tensor": lax.rem(t + j, tensors)},
                device_id_type=MESH,
            )

        for j in range(1, tensors):
            copy_c(j).start()

        @pl.when(target != g)
        def _():
            copy_c(0).start()

        @pl.when(target == g)
        def _():
            pltpu.make_async_copy(send_c.at[h], recv_c.at[slot], recv_sem.at[2]).start()

    whole(recv_c, recv_sem.at[2]).wait()
    hidden = recv_a[...].astype(F32) + recv_c[...].astype(F32)
    square = jnp.sum(hidden * hidden, axis=2, keepdims=True)
    square = square[:, :ROWS] + square[:, ROWS:]
    products = project(1, hidden)
    products = jnp.concatenate(
        [products, jnp.broadcast_to(square, (groups, ROWS, HD))], axis=2
    )
    send_d[...] = products
    to_group(send_d, recv_d, 3, -1, True)
    recv_d[0] = products[0]
    own = stack_rows(own_v[...])

    whole(recv_d.at[rest], recv_sem.at[3]).wait()
    summed = jnp.sum(recv_d[...], axis=0)
    scale_1 = lax.rsqrt(summed[:, 2 * HD : 2 * HD + 1] / width + 1e-05)
    attended_1 = merge(summed[:, : 2 * HD] * scale_1, part_1)
    for i in range(QPK):
        at = slice(i * HD, (i + 1) * HD)
        out[:, at] = own[:, at] + attended_0[i] + attended_1[i]

    for phase, src in ((0, send_a), (1, send_b), (3, send_d)):
        whole(src.at[rest], send_sem.at[phase]).wait()

    @pl.when(home != t)
    def _():
        whole(recv_c, send_sem.at[2]).wait()

    @pl.when(home == t)
    def _():
        whole(recv_c.at[rest], send_sem.at[2]).wait()


def solution(mesh):
    groups, tensors = mesh.shape["group"], mesh.shape["tensor"]

    def per_device(tokens, queries, cache_kv, old_kv, new_kv, switch, lengths):
        depth = new_kv.shape[1]
        half = depth // 2
        block = tokens.shape[2] // tensors
        cache_len = cache_kv.shape[2]
        hbm = pl.BlockSpec(memory_space=pltpu.HBM)
        vmem = pltpu.VMEM
        result = pl.pallas_call(
            functools.partial(kernel, groups, tensors),
            out_shape=jax.ShapeDtypeStruct((ROWS, block), F32),
            in_specs=[hbm] * 7,
            out_specs=pl.BlockSpec(memory_space=vmem),
            scratch_shapes=[
                pltpu.SMEM(switch.shape, jnp.int32),
                pltpu.SMEM(lengths.shape, jnp.int32),
                vmem(tokens.shape, BF16),
                vmem((STEPS, SEQS, block), BF16),
                vmem(queries.shape, BF16),
                vmem((LAYERS, 2, cache_len, 2 * HD), BF16),
                vmem((LAYERS, 2, SHORT, 2 * HD), BF16),
                vmem(new_kv.shape, BF16),
                vmem(new_kv.shape, BF16),
                vmem((groups, 2 * ROWS, half), BF16),
                vmem((groups, 2 * ROWS, half), BF16),
                vmem((groups, ROWS, 2 * HD), F32),
                vmem((groups, ROWS, 2 * HD), F32),
                vmem((2, 2 * ROWS, half), BF16),
                vmem((groups, 2 * ROWS, half), BF16),
                vmem((groups, ROWS, 3 * HD), F32),
                vmem((groups, ROWS, 3 * HD), F32),
                pltpu.SemaphoreType.DMA((7,)),
                pltpu.SemaphoreType.DMA((LAYERS, 2)),
                pltpu.SemaphoreType.DMA((LAYERS, 2)),
                pltpu.SemaphoreType.DMA((4,)),
                pltpu.SemaphoreType.DMA((4,)),
            ],
            compiler_params=pltpu.CompilerParams(
                collective_id=0, has_side_effects=True, vmem_limit_bytes=40 * 2**20
            ),
        )(tokens, queries, cache_kv, old_kv, new_kv, switch, lengths)
        return result.astype(BF16).reshape(STEPS, SEQS, block)

    return jax.shard_map(
        per_device,
        mesh=mesh,
        in_specs=(
            P(None, "group", None),
            P(None, None, "group", "tensor"),
            P(None, "group", None, "tensor"),
            P(None, None, "tensor"),
            P(None, "group", "tensor"),
            P(),
            P("group"),
        ),
        out_specs=P(None, "group", "tensor"),
        check_vma=False,
    )
```

time: 107 us -> 44.7 us (0.42)
  the two profiles are of different devices: /device:TPU:0 before, /device:TPU:1 now
where the time goes in v1:
time: 44.7 us; the launch traced here: 44.4 us
  Pallas kernels  36.3 us (81%)
  local copies, waits for them, and re-layouts  8.01 us (18%)
    pallas_call x1, Pallas kernels, per_device(): pl.pallas_call(functools.partial(kernel, groups, tensors), out_shape=jax....  36.3 us
    unnamed x12, local copies, waits for them, and re-layouts  7.39 us

profile of v1, /device:TPU:1, one launch (start us, length us, event | category | flops | bytes accessed | tf_op | source)
XLA Modules:
  0.0 44.4 jit_solution(17153146592689504214)
XLA Ops:
  0.0 0.0 copy-start
  0.0 3.4 %copy-done = bf16[2,4,2048,256]{3,2,1,0:T(8,128)(2,1)S(1)} copy-done((bf16[2,4,2048,256]{3,2,1,0:T(8,128)(2,1)S(1)}, bf16[2,4,2048,256]{3,2,1,0:T(8,128)(2,1)}, u32[]{:S(2)}) %copy-start) | copy-done | bytes 8388632
  3.4 0.0 copy-start.1
  3.4 1.0 %copy-done.1 = bf16[2,512,256]{2,1,0:T(8,128)(2,1)S(1)} copy-done((bf16[2,512,256]{2,1,0:T(8,128)(2,1)S(1)}, bf16[2,512,256]{2,1,0:T(8,128)(2,1)}, u32[]{:S(2)}) %copy-start.1) | copy-done | bytes 524312
  4.4 0.0 copy-start.2
  4.4 0.9 %copy-done.2 = bf16[2,4,8192]{2,1,0:T(4,128)(2,1)S(1)} copy-done((bf16[2,4,8192]{2,1,0:T(4,128)(2,1)S(1)}, bf16[2,4,8192]{2,1,0:T(4,128)(2,1)}, u32[]{:S(2)}) %copy-start.2) | copy-done | bytes 131096
  5.3 0.0 copy-start.3
  5.3 0.8 %copy-done.3 = bf16[2,2,4,1024]{3,2,1,0:T(4,128)(2,1)S(1)} copy-done((bf16[2,2,4,1024]{3,2,1,0:T(4,128)(2,1)S(1)}, bf16[2,2,4,1024]{3,2,1,0:T(4,128)(2,1)}, u32[]{:S(2)}) %copy-start.3) | copy-done | bytes 32792
  6.1 0.0 copy-start.4
  6.1 0.7 %copy-done.4 = s32[2]{0:T(128)S(1)} copy-done((s32[2]{0:T(128)S(1)}, s32[2]{0:T(128)}, u32[]{:S(2)}) %copy-start.4) | copy-done | bytes 32
  6.7 0.0 copy-start.5
  6.7 0.7 %copy-done.5 = s32[4]{0:T(128)S(1)} copy-done((s32[4]{0:T(128)S(1)}, s32[4]{0:T(128)}, u32[]{:S(2)}) %copy-start.5) | copy-done | bytes 40
  7.4 36.3 %shard_map.73 = f32[8,1024]{1,0:T(8,128)S(1)} custom-call(bf16[2,4,8192]{2,1,0:T(4,128)(2,1)S(1)} %copy-done.2, bf16[2,2,4,1024]{3,2,1,0:T(4,128)(2,1)S(1)} %copy-done.3, bf16[2,4,2048,256]{3,2,1,0:T(8,128)(2,1)S(1)} %copy-done, bf16[2,8192,256]{2,1,0:T(8,128)(2,1)} %old_kv.1, bf16[2,512,256]{2,1,0:T(8,128)(2,1)S(1)} %copy-done.1, s32[2]{0:T(128)S(1)} %copy-done.4, ...), custom_call_target="tpu_custom_call" | custom-call | tf_op jit(solution)/shard_map/pallas_call | solution.py:331
  43.7 0.6 %reshape.3 = bf16[2,4,1024]{2,1,0:T(4,128)(2,1)} reshape(bf16[8,1024]{1,0:T(8,128)(2,1)S(1)} %convert_element_type.3) | data formatting | bytes 32768 | tf_op jit(solution)/shard_map/reshape | solution.py:364
  (1 shorter events, 0.0 us)
Async XLA Ops:
  0.0 3.4 %copy-start = (bf16[2,4,2048,256]{3,2,1,0:T(8,128)(2,1)S(1)}, bf16[2,4,2048,256]{3,2,1,0:T(8,128)(2,1)}, u32[]{:S(2)}) copy-start(bf16[2,4,2048,256]{3,2,1,0:T(8,128)(2,1)} %cache.1) | copy-start | bytes 25165828
  3.4 1.0 %copy-start.1 = (bf16[2,512,256]{2,1,0:T(8,128)(2,1)S(1)}, bf16[2,512,256]{2,1,0:T(8,128)(2,1)}, u32[]{:S(2)}) copy-start(bf16[2,512,256]{2,1,0:T(8,128)(2,1)} %new_kv.1) | copy-start | bytes 1572868
  4.4 0.9 %copy-start.2 = (bf16[2,4,8192]{2,1,0:T(4,128)(2,1)S(1)}, bf16[2,4,8192]{2,1,0:T(4,128)(2,1)}, u32[]{:S(2)}) copy-start(bf16[2,4,8192]{2,1,0:T(4,128)(2,1)} %tokens.1) | copy-start | bytes 393220
  5.3 0.8 %copy-start.3 = (bf16[2,2,4,1024]{3,2,1,0:T(4,128)(2,1)S(1)}, bf16[2,2,4,1024]{3,2,1,0:T(4,128)(2,1)}, u32[]{:S(2)}) copy-start(bf16[2,2,4,1024]{3,2,1,0:T(4,128)(2,1)} %queries.1) | copy-start | bytes 98308
  6.1 0.7 %copy-start.4 = (s32[2]{0:T(128)S(1)}, s32[2]{0:T(128)}, u32[]{:S(2)}) copy-start(s32[2]{0:T(128)} %switch_hbm.1) | copy-start | bytes 28
  6.7 0.7 %copy-start.5 = (s32[4]{0:T(128)S(1)}, s32[4]{0:T(128)}, u32[]{:S(2)}) copy-start(s32[4]{0:T(128)} %lengths_hbm.1) | copy-start | bytes 52

commit v2 on v1

--- a/solution.py
+++ b/solution.py
@@ -44,14 +44,17 @@
     q_v,
     long_v,
     short_v,
-    old_v,
-    new_v,
+    old_0,
+    old_1,
+    new_0,
+    new_1,
     send_a,
     recv_a,
     send_b,
     recv_b,
     send_c,
     recv_c,
+    recv_t,
     send_d,
     recv_d,
     load_sem,
@@ -66,29 +69,40 @@
     half = depth // 2
     width = tokens.shape[2]
     block = width // tensors
-    home = g // 2
+    x, y, core = g // 4, lax.rem(g // 2, 2), lax.rem(g, 2)
+
+    def device(group, tensor):
+        return {"group": group, "tensor": tensor}
+
+    def holder(row_block, column_block):
+        across = lax.rem(row_block // 4 + column_block // 2, 4)
+        along = lax.rem(row_block // 2 + column_block, 2)
+        return 4 * across + 2 * along + lax.rem(row_block, 2)
+
+    there = device(holder(g, t), g // 2)
+    column = 2 * lax.rem(x + 4 - t // 2, 4) + lax.rem(y + t, 2)
+    origin = device(2 * t + core, column)
+
+    def same(other):
+        return (other["group"] == g) & (other["tensor"] == t)
 
     barrier = pltpu.get_barrier_semaphore()
+
+    def greet(other):
+        pl.semaphore_signal(barrier, inc=1, device_id=other, device_id_type=MESH)
+
+    def greet_other(other):
+        @pl.when(jnp.logical_not(same(other)))
+        def _():
+            greet(other)
+
     for k in range(1, groups):
-        pl.semaphore_signal(
-            barrier,
-            inc=1,
-            device_id={"group": lax.rem(g + k, groups), "tensor": t},
-            device_id_type=MESH,
-        )
-    for k in range(1, groups):
-        pl.semaphore_signal(
-            barrier,
-            inc=1,
-            device_id={"group": lax.rem(g + k, groups), "tensor": home},
-            device_id_type=MESH,
-        )
-
-    @pl.when(home != t)
-    def _():
-        pl.semaphore_signal(
-            barrier, inc=1, device_id={"group": g, "tensor": home}, device_id_type=MESH
-        )
+        greet(device(lax.rem(g + k, groups), t))
+    for k in range(1, tensors):
+        greet(device(g, lax.rem(t + k, tensors)))
+    greet_other(origin)
+    for block_index in range(groups):
+        greet_other(device(holder(block_index, t), block_index // 2))
 
     loads = [
         pltpu.make_async_copy(tokens, tok_v, load_sem.at[0]),
@@ -98,15 +112,16 @@
             load_sem.at[1],
         ),
         pltpu.make_async_copy(queries, q_v, load_sem.at[2]),
-        pltpu.make_async_copy(new_kv, new_v, load_sem.at[3]),
+        pltpu.make_async_copy(new_kv.at[0], new_0, load_sem.at[3]),
         pltpu.make_async_copy(
-            old_kv.at[:, pl.ds(pl.multiple_of(g * depth, depth), depth), :],
-            old_v,
+            old_kv.at[0, pl.ds(pl.multiple_of(g * depth, depth), depth), :],
+            old_0,
             load_sem.at[4],
         ),
         pltpu.make_async_copy(switch_hbm, switch, load_sem.at[5]),
         pltpu.make_async_copy(lengths_hbm, lengths, load_sem.at[6]),
     ]
+    late = pltpu.make_async_copy(old_kv.at[1], old_1, load_sem.at[7])
     longs = [
         [
             pltpu.make_async_copy(
@@ -133,6 +148,7 @@
         for j in range(2):
             longs[layer][j].start()
             shorts[layer][j].start()
+    late.start()
 
     loads[0].wait()
     mine = stack_rows(tok_v[...])
@@ -141,13 +157,9 @@
         send_a[k] = jnp.concatenate([piece[:, :half], piece[:, half:]], axis=0).astype(BF16)
     scale_0 = lax.rsqrt(jnp.sum(mine * mine, axis=1, keepdims=True) / width + 1e-05)
 
-    @pl.when(home != t)
-    def _():
-        pl.semaphore_wait(barrier, 2 * groups - 1)
-
-    @pl.when(home == t)
-    def _():
-        pl.semaphore_wait(barrier, 2 * groups - 2)
+    waited = groups - 1 + tensors - 1 + 1 + groups
+    stays = same(there).astype(jnp.int32) + (column == t).astype(jnp.int32)
+    pl.semaphore_wait(barrier, waited - stays)
 
     def whole(ref, sem):
         return pltpu.make_async_copy(ref, ref, sem)
@@ -166,6 +178,24 @@
 
     to_group(send_a, recv_a, 0, 1, False)
     recv_a[0] = send_a[g]
+
+    def put(src, dst, other, phase):
+        @pl.when(jnp.logical_not(same(other)))
+        def _():
+            pltpu.make_async_remote_copy(
+                src_ref=src,
+                dst_ref=dst,
+                send_sem=send_sem.at[phase],
+                recv_sem=recv_sem.at[phase],
+                device_id=other,
+                device_id_type=MESH,
+            ).start()
+
+        @pl.when(same(other))
+        def _():
+            pltpu.make_async_copy(src, dst, recv_sem.at[phase]).start()
+
+    put(new_kv.at[1], new_1, there, 4)
 
     row = lax.broadcasted_iota(jnp.int32, (QPK * ROWS, 1), 0)
     row_seq = lax.rem(row, SEQS)
@@ -226,15 +256,10 @@
         result = (mixed * keep + w_0 * value_0[None] + w_1 * value_1[None]) * norm
         return result.astype(BF16).astype(F32)
 
-    def project(layer, features):
-        flat = jnp.concatenate(
+    def flatten(features):
+        return jnp.concatenate(
             [features[:, :ROWS].reshape(-1, half), features[:, ROWS:].reshape(-1, half)], axis=1
         ).astype(BF16)
-        by_new = jnp.dot(flat, new_v[layer], preferred_element_type=F32)
-        by_old = jnp.dot(flat, old_v[layer], preferred_element_type=F32)
-        step = lax.rem(lax.broadcasted_iota(jnp.int32, by_new.shape, 0), ROWS) // SEQS
-        picked = jnp.where(step >= switch[layer], by_new, by_old)
-        return picked.reshape(groups, ROWS, -1)
 
     for copy in loads[1:]:
         copy.wait()
@@ -242,7 +267,11 @@
 
     rest = pl.ds(1, groups - 1)
     whole(recv_a.at[rest], recv_sem.at[0]).wait()
-    products = project(0, recv_a[...].astype(F32))
+    flat = flatten(recv_a[...].astype(F32))
+    by_new = jnp.dot(flat, new_0[...], preferred_element_type=F32)
+    by_old = jnp.dot(flat, old_0[...], preferred_element_type=F32)
+    step = lax.rem(lax.broadcasted_iota(jnp.int32, by_new.shape, 0), ROWS) // SEQS
+    products = jnp.where(step >= switch[0], by_new, by_old).reshape(groups, ROWS, -1)
     send_b[...] = products
     to_group(send_b, recv_b, 1, -1, True)
     recv_b[0] = products[0]
@@ -250,72 +279,73 @@
 
     whole(recv_b.at[rest], recv_sem.at[1]).wait()
     attended_0 = merge(jnp.sum(recv_b[...], axis=0) * scale_0, part_0)
-    pair = QPK // 4
+    own = stack_rows(own_v[...])
+    hidden = [own[:, i * HD : (i + 1) * HD] + attended_0[i] for i in range(QPK)]
     for h in range(2):
         send_c[h] = jnp.concatenate(
-            [
-                jnp.concatenate([attended_0[4 * h + 2 * r + c] for c in range(pair)], axis=1)
-                for r in range(2)
-            ],
+            [jnp.concatenate(hidden[4 * h + 2 * r : 4 * h + 2 * r + 2], axis=1) for r in range(2)],
             axis=0,
         ).astype(BF16)
 
-    for h in range(2):
-        target = 2 * t + h
-        slot = lax.rem(target + groups - g, groups)
-
-        def copy_c(j):
-            return pltpu.make_async_remote_copy(
-                src_ref=send_c.at[h],
-                dst_ref=recv_c.at[slot],
-                send_sem=send_sem.at[2],
-                recv_sem=recv_sem.at[2],
-                device_id={"group": target, "tensor": lax.rem(t + j, tensors)},
-                device_id_type=MESH,
-            )
-
-        for j in range(1, tensors):
-            copy_c(j).start()
-
-        @pl.when(target != g)
-        def _():
-            copy_c(0).start()
-
-        @pl.when(target == g)
-        def _():
-            pltpu.make_async_copy(send_c.at[h], recv_c.at[slot], recv_sem.at[2]).start()
-
+    for k in range(1, groups):
+        peer = lax.rem(g + k, groups)
+        pltpu.make_async_remote_copy(
+            src_ref=send_c.at[lax.rem(peer, 2)],
+            dst_ref=recv_c.at[g],
+            send_sem=send_sem.at[2],
+            recv_sem=recv_sem.at[2],
+            device_id=device(peer, t),
+            device_id_type=MESH,
+        ).start()
+    pltpu.make_async_copy(send_c.at[core], recv_c.at[g], recv_sem.at[2]).start()
+    for k in range(1, tensors):
+        pltpu.make_async_remote_copy(
+            src_ref=send_c,
+            dst_ref=recv_t.at[t],
+            send_sem=send_sem.at[5],
+            recv_sem=recv_sem.at[5],
+            device_id=device(g, lax.rem(t + k, tensors)),
+            device_id_type=MESH,
+        ).start()
+    pltpu.make_async_copy(send_c, recv_t.at[t], recv_sem.at[5]).start()
+
+    whole(new_1, recv_sem.at[4]).wait()
     whole(recv_c, recv_sem.at[2]).wait()
-    hidden = recv_a[...].astype(F32) + recv_c[...].astype(F32)
-    square = jnp.sum(hidden * hidden, axis=2, keepdims=True)
-    square = square[:, :ROWS] + square[:, ROWS:]
-    products = project(1, hidden)
-    products = jnp.concatenate(
-        [products, jnp.broadcast_to(square, (groups, ROWS, HD))], axis=2
-    )
-    send_d[...] = products
-    to_group(send_d, recv_d, 3, -1, True)
-    recv_d[0] = products[0]
-    own = stack_rows(own_v[...])
-
-    whole(recv_d.at[rest], recv_sem.at[3]).wait()
-    summed = jnp.sum(recv_d[...], axis=0)
-    scale_1 = lax.rsqrt(summed[:, 2 * HD : 2 * HD + 1] / width + 1e-05)
-    attended_1 = merge(summed[:, : 2 * HD] * scale_1, part_1)
+    flat = flatten(recv_c[...].astype(F32))
+    send_d[...] = jnp.dot(flat, new_1[...], preferred_element_type=F32).reshape(groups, ROWS, -1)
+    for k in range(groups):
+        peer = lax.rem(g + k, groups)
+        put(send_d.at[peer], recv_d.at[2 * t + core], device(peer, column), 3)
+
+    late.wait()
+    whole(recv_t, recv_sem.at[5]).wait()
+    parts = [recv_t[i, h].astype(F32) for i in range(tensors) for h in range(2)]
+    wide = jnp.concatenate([part[at : at + ROWS] for part in parts for at in (0, ROWS)], axis=1)
+    scale_1 = lax.rsqrt(jnp.sum(wide * wide, axis=1, keepdims=True) / width + 1e-05)
+    by_old = jnp.dot(wide.astype(BF16), old_1[...], preferred_element_type=F32)
+    row_step = lax.broadcasted_iota(jnp.int32, by_old.shape, 0) // SEQS
+
+    whole(recv_d, recv_sem.at[3]).wait()
+    summed = jnp.where(row_step >= switch[1], jnp.sum(recv_d[...], axis=0), by_old)
+    attended_1 = merge(summed * scale_1, part_1)
     for i in range(QPK):
-        at = slice(i * HD, (i + 1) * HD)
-        out[:, at] = own[:, at] + attended_0[i] + attended_1[i]
-
-    for phase, src in ((0, send_a), (1, send_b), (3, send_d)):
+        out[:, i * HD : (i + 1) * HD] = hidden[i] + attended_1[i]
+
+    for phase, src in ((0, send_a), (1, send_b), (2, recv_c)):
         whole(src.at[rest], send_sem.at[phase]).wait()
-
-    @pl.when(home != t)
+    whole(recv_t.at[pl.ds(1, tensors - 1)], send_sem.at[5]).wait()
+
+    @pl.when(jnp.logical_not(same(there)))
     def _():
-        whole(recv_c, send_sem.at[2]).wait()
-
-    @pl.when(home == t)
+        whole(new_1, send_sem.at[4]).wait()
+
+    @pl.when(column != t)
     def _():
-        whole(recv_c.at[rest], send_sem.at[2]).wait()
+        whole(send_d, send_sem.at[3]).wait()
+
+    @pl.when(column == t)
+    def _():
+        whole(send_d.at[rest], send_sem.at[3]).wait()
 
 
 def solution(mesh):
@@ -341,24 +371,27 @@
                 vmem(queries.shape, BF16),
                 vmem((LAYERS, 2, cache_len, 2 * HD), BF16),
                 vmem((LAYERS, 2, SHORT, 2 * HD), BF16),
-                vmem(new_kv.shape, BF16),
-                vmem(new_kv.shape, BF16),
+                vmem((depth, 2 * HD), BF16),
+                vmem(old_kv.shape[1:], BF16),
+                vmem((depth, 2 * HD), BF16),
+                vmem((depth, 2 * HD), BF16),
                 vmem((groups, 2 * ROWS, half), BF16),
                 vmem((groups, 2 * ROWS, half), BF16),
                 vmem((groups, ROWS, 2 * HD), F32),
                 vmem((groups, ROWS, 2 * HD), F32),
                 vmem((2, 2 * ROWS, half), BF16),
                 vmem((groups, 2 * ROWS, half), BF16),
-                vmem((groups, ROWS, 3 * HD), F32),
-                vmem((groups, ROWS, 3 * HD), F32),
-                pltpu.SemaphoreType.DMA((7,)),
+                vmem((tensors, 2, 2 * ROWS, half), BF16),
+                vmem((groups, ROWS, 2 * HD), F32),
+                vmem((groups, ROWS, 2 * HD), F32),
+                pltpu.SemaphoreType.DMA((8,)),
                 pltpu.SemaphoreType.DMA((LAYERS, 2)),
                 pltpu.SemaphoreType.DMA((LAYERS, 2)),
-                pltpu.SemaphoreType.DMA((4,)),
-                pltpu.SemaphoreType.DMA((4,)),
+                pltpu.SemaphoreType.DMA((6,)),
+                pltpu.SemaphoreType.DMA((6,)),
             ],
             compiler_params=pltpu.CompilerParams(
-                collective_id=0, has_side_effects=True, vmem_limit_bytes=40 * 2**20
+                collective_id=0, has_side_effects=True, vmem_limit_bytes=56 * 2**20
             ),
         )(tokens, queries, cache_kv, old_kv, new_kv, switch, lengths)
         return result.astype(BF16).reshape(STEPS, SEQS, block)

time: 44.7 us -> 36.2 us (0.81)
  local copies, waits for them, and re-layouts: 8.01 us -> 0.62 us
  Pallas kernels: 36.3 us -> 34.7 us
  other arithmetic: 0.01 us -> 0.76 us
    unnamed x12 -> x0, local copies, waits for them, and re-layouts: 7.39 us -> none
    pallas_call x1, Pallas kernels: 36.3 us -> 34.7 us  [per_device(): pl.pallas_call(functools.partial(kernel, groups, tensors), out_shape=jax....]
    convert_element_type x1, other arithmetic: 0.01 us -> 0.76 us  [per_device(): return result.astype(BF16).reshape(STEPS, SEQS, block)]
where the time goes in v2:
time: 36.2 us; the launch traced here: 36.1 us
  Pallas kernels  34.7 us (96%)
  other arithmetic  0.76 us (2%)
  local copies, waits for them, and re-layouts  0.62 us (2%)
    pallas_call x1, Pallas kernels, per_device(): pl.pallas_call(functools.partial(kernel, groups, tensors), out_shape=jax....  34.7 us
    convert_element_type x1, other arithmetic, per_device(): return result.astype(BF16).reshape(STEPS, SEQS, block)  0.76 us

profile of v2, /device:TPU:1, one launch (start us, length us, event | category | flops | bytes accessed | tf_op | source)
XLA Modules:
  0.0 36.1 jit_solution(5551325847079927875)
XLA Ops:
  0.0 34.7 %shard_map.73 = f32[8,1024]{1,0:T(8,128)} custom-call(bf16[2,4,8192]{2,1,0:T(4,128)(2,1)} %tokens.1, bf16[2,2,4,1024]{3,2,1,0:T(4,128)(2,1)} %queries.1, bf16[2,4,2048,256]{3,2,1,0:T(8,128)(2,1)} %cache.1, bf16[2,8192,256]{2,1,0:T(8,128)(2,1)} %old_kv.1, bf16[2,512,256]{2,1,0:T(8,128)(2,1)} %new_kv.1, s32[2]{0:T(128)} %switch_hbm.1, s32[4]{0:T(128)} %lengths_hbm.1), custom_call_target="tpu_custom_call" | custom-call | tf_op jit(solution)/shard_map/pallas_call | solution.py:361
  34.7 0.8 %convert_element_type.3 = bf16[8,1024]{1,0:T(8,128)(2,1)S(1)} convert(f32[8,1024]{1,0:T(8,128)} %shard_map.73) | non-fusion elementwise | flops 8192 | bytes 49152 | tf_op jit(solution)/shard_map/convert_element_type | solution.py:397
  35.5 0.6 %reshape.3 = bf16[2,4,1024]{2,1,0:T(4,128)(2,1)} reshape(bf16[8,1024]{1,0:T(8,128)(2,1)S(1)} %convert_element_type.3) | data formatting | bytes 32768 | tf_op jit(solution)/shard_map/reshape | solution.py:397

commit v3 on v2

--- a/solution.py
+++ b/solution.py
@@ -62,6 +62,8 @@
     short_sem,
     send_sem,
     recv_sem,
+    near_sem,
+    far_sem,
 ):
     g = lax.axis_index("group")
     t = lax.axis_index("tensor")
@@ -75,34 +77,55 @@
         return {"group": group, "tensor": tensor}
 
     def holder(row_block, column_block):
-        across = lax.rem(row_block // 4 + column_block // 2, 4)
-        along = lax.rem(row_block // 2 + column_block, 2)
-        return 4 * across + 2 * along + lax.rem(row_block, 2)
-
-    there = device(holder(g, t), g // 2)
-    column = 2 * lax.rem(x + 4 - t // 2, 4) + lax.rem(y + t, 2)
+        side = lax.rem(row_block, 2)
+        across = lax.rem(row_block // 4 + column_block // 2 + 2 * side, 4)
+        along = lax.rem(row_block // 2 + column_block + side, 2)
+        return 4 * across + 2 * along + side
+
+    def route(side):
+        goes = device(holder(2 * (g // 2) + side, t), g // 2)
+        return goes, 2 * lax.rem(x + 8 - t // 2 - 2 * side, 4) + lax.rem(y + t + side, 2)
+
+    def targets(side):
+        goes, columns = route(side)
+        yield goes
+        for group in range(groups):
+            yield device(group, columns)
+
+    there, column = route(core)
     origin = device(2 * t + core, column)
 
     def same(other):
         return (other["group"] == g) & (other["tensor"] == t)
 
     barrier = pltpu.get_barrier_semaphore()
+    mate = device(g + 1 - 2 * core, t)
 
     def greet(other):
         pl.semaphore_signal(barrier, inc=1, device_id=other, device_id_type=MESH)
 
-    def greet_other(other):
-        @pl.when(jnp.logical_not(same(other)))
+    def same_chip(other):
+        return (other["group"] // 2 == g // 2) & (other["tensor"] == t)
+
+    def senders():
+        yield origin
+        for block_index in range(groups):
+            yield device(holder(block_index, t), block_index // 2)
+
+    for k in range(1, groups // 2):
+        greet(device(2 * lax.rem(g // 2 + k, groups // 2), t))
+
+    @pl.when(core == 1)
+    def _():
+        greet(mate)
+
+    for k in range(1, tensors):
+        greet(device(g - core + 1, lax.rem(t + k, tensors)))
+    for other in senders():
+
+        @pl.when(jnp.logical_not(same_chip(other)))
         def _():
-            greet(other)
-
-    for k in range(1, groups):
-        greet(device(lax.rem(g + k, groups), t))
-    for k in range(1, tensors):
-        greet(device(g, lax.rem(t + k, tensors)))
-    greet_other(origin)
-    for block_index in range(groups):
-        greet_other(device(holder(block_index, t), block_index // 2))
+            greet(device(2 * (other["group"] // 2) + 1, other["tensor"]))
 
     loads = [
         pltpu.make_async_copy(tokens, tok_v, load_sem.at[0]),
@@ -157,9 +180,29 @@
         send_a[k] = jnp.concatenate([piece[:, :half], piece[:, half:]], axis=0).astype(BF16)
     scale_0 = lax.rsqrt(jnp.sum(mine * mine, axis=1, keepdims=True) / width + 1e-05)
 
-    waited = groups - 1 + tensors - 1 + 1 + groups
-    stays = same(there).astype(jnp.int32) + (column == t).astype(jnp.int32)
-    pl.semaphore_wait(barrier, waited - stays)
+    @pl.when(core == 0)
+    def _():
+        pl.semaphore_wait(barrier, groups - 1)
+        pl.semaphore_signal(near_sem, inc=1, device_id=mate, device_id_type=MESH)
+
+    @pl.when(core == 1)
+    def _():
+        pl.semaphore_wait(near_sem, 1)
+
+    def far_barrier():
+        count = 2 * (tensors - 1)
+        for other_core in range(2):
+            for other in targets(other_core):
+                count = count + jnp.logical_not(same_chip(other)).astype(jnp.int32)
+
+        @pl.when(core == 1)
+        def _():
+            pl.semaphore_wait(barrier, count)
+            pl.semaphore_signal(far_sem, inc=1, device_id=mate, device_id_type=MESH)
+
+        @pl.when(core == 0)
+        def _():
+            pl.semaphore_wait(far_sem, 1)
 
     def whole(ref, sem):
         return pltpu.make_async_copy(ref, ref, sem)
@@ -195,6 +238,7 @@
         def _():
             pltpu.make_async_copy(src, dst, recv_sem.at[phase]).start()
 
+    far_barrier()
     put(new_kv.at[1], new_1, there, 4)
 
     row = lax.broadcasted_iota(jnp.int32, (QPK * ROWS, 1), 0)
@@ -329,7 +373,9 @@
     summed = jnp.where(row_step >= switch[1], jnp.sum(recv_d[...], axis=0), by_old)
     attended_1 = merge(summed * scale_1, part_1)
     for i in range(QPK):
-        out[:, i * HD : (i + 1) * HD] = hidden[i] + attended_1[i]
+        rows = (hidden[i] + attended_1[i]).astype(BF16)
+        out[0, :, i * HD : (i + 1) * HD] = rows[:SEQS]
+        out[1, :, i * HD : (i + 1) * HD] = rows[SEQS:]
 
     for phase, src in ((0, send_a), (1, send_b), (2, recv_c)):
         whole(src.at[rest], send_sem.at[phase]).wait()
@@ -360,7 +406,7 @@
         vmem = pltpu.VMEM
         result = pl.pallas_call(
             functools.partial(kernel, groups, tensors),
-            out_shape=jax.ShapeDtypeStruct((ROWS, block), F32),
+            out_shape=jax.ShapeDtypeStruct((STEPS, SEQS, block), BF16),
             in_specs=[hbm] * 7,
             out_specs=pl.BlockSpec(memory_space=vmem),
             scratch_shapes=[
@@ -389,12 +435,14 @@
                 pltpu.SemaphoreType.DMA((LAYERS, 2)),
                 pltpu.SemaphoreType.DMA((6,)),
                 pltpu.SemaphoreType.DMA((6,)),
+                pltpu.SemaphoreType.REGULAR,
+                pltpu.SemaphoreType.REGULAR,
             ],
             compiler_params=pltpu.CompilerParams(
                 collective_id=0, has_side_effects=True, vmem_limit_bytes=56 * 2**20
             ),
         )(tokens, queries, cache_kv, old_kv, new_kv, switch, lengths)
-        return result.astype(BF16).reshape(STEPS, SEQS, block)
+        return result
 
     return jax.shard_map(
         per_device,

time: 36.2 us -> 32 us (0.88)
  Pallas kernels: 34.7 us -> 30.5 us
  other arithmetic: 0.76 us -> 0 us
  local copies, waits for them, and re-layouts: 0.62 us -> 1.33 us
    pallas_call x1, Pallas kernels: 34.7 us -> 30.5 us  [per_device(): pl.pallas_call(functools.partial(kernel, groups, tensors), out_shape=jax....]
    unnamed x0 -> x1, local copies, waits for them, and re-layouts: none -> 1.33 us
    convert_element_type x1 -> x0, other arithmetic: 0.76 us -> none  [per_device(): return result.astype(BF16).reshape(STEPS, SEQS, block)]
    reshape x1 -> x0, local copies, waits for them, and re-layouts: 0.62 us -> none  [per_device(): return result.astype(BF16).reshape(STEPS, SEQS, block)]
where the time goes in v3:
time: 32 us; the launch traced here: 31.8 us
  Pallas kernels  30.5 us (95%)
  local copies, waits for them, and re-layouts  1.33 us (4%)
    pallas_call x1, Pallas kernels, per_device(): pl.pallas_call(functools.partial(kernel, groups, tensors), out_shape=jax....  30.5 us
    unnamed x1, local copies, waits for them, and re-layouts  1.33 us

profile of v3, /device:TPU:1, one launch (start us, length us, event | category | flops | bytes accessed | tf_op | source)
XLA Modules:
  0.0 31.8 jit_solution(2213044912241996597)
XLA Ops:
  0.0 30.5 %shard_map.73 = bf16[2,4,1024]{2,1,0:T(4,128)(2,1)} custom-call(bf16[2,4,8192]{2,1,0:T(4,128)(2,1)} %tokens.1, bf16[2,2,4,1024]{3,2,1,0:T(4,128)(2,1)} %queries.1, bf16[2,4,2048,256]{3,2,1,0:T(8,128)(2,1)} %cache.1, bf16[2,8192,256]{2,1,0:T(8,128)(2,1)} %old_kv.1, bf16[2,512,256]{2,1,0:T(8,128)(2,1)} %new_kv.1, s32[2]{0:T(128)} %switch_hbm.1, s32[4]{0:T(128)} %lengths_hbm.1), custom_call_target="tpu_custom_call" | custom-call | tf_op jit(solution)/shard_map/pallas_call | solution.py:407
  30.5 1.3 %copy.9 = bf16[2,4,1024]{2,1,0:T(4,128)(2,1)} copy(bf16[2,4,1024]{2,1,0:T(4,128)(2,1)} %shard_map.73) | data formatting | bytes 32768

commit v4 on v3

--- a/solution.py
+++ b/solution.py
@@ -284,11 +284,10 @@
         other = jnp.concatenate([fresh[SEQS:], fresh[:SEQS]], axis=0)
         return jnp.where(upper, fresh, other), jnp.where(upper, other, fresh)
 
-    def merge(fresh, part):
+    def merge(key, value, part):
         q, top, total, mixed = part
-        fresh = fresh.astype(BF16).astype(F32)
-        key_0, key_1 = by_step(fresh[:, :HD])
-        value_0, value_1 = by_step(fresh[:, HD:])
+        key_0, key_1 = by_step(key.astype(BF16).astype(F32))
+        value_0, value_1 = by_step(value.astype(BF16).astype(F32))
         s_0 = jnp.sum(q * key_0[None], axis=2, keepdims=True) * UNIT
         s_1 = jnp.sum(q * key_1[None], axis=2, keepdims=True) * UNIT
         s_1 = jnp.where(upper[None, :, :1], FAR, s_1)
@@ -300,6 +299,10 @@
         result = (mixed * keep + w_0 * value_0[None] + w_1 * value_1[None]) * norm
         return result.astype(BF16).astype(F32)
 
+    def fold(products):
+        products = products.reshape(groups, ROWS, 2 * HD)
+        return jnp.concatenate([products[:, :, :HD], products[:, :, HD:]], axis=1).astype(BF16)
+
     def flatten(features):
         return jnp.concatenate(
             [features[:, :ROWS].reshape(-1, half), features[:, ROWS:].reshape(-1, half)], axis=1
@@ -315,14 +318,14 @@
     by_new = jnp.dot(flat, new_0[...], preferred_element_type=F32)
     by_old = jnp.dot(flat, old_0[...], preferred_element_type=F32)
     step = lax.rem(lax.broadcasted_iota(jnp.int32, by_new.shape, 0), ROWS) // SEQS
-    products = jnp.where(step >= switch[0], by_new, by_old).reshape(groups, ROWS, -1)
-    send_b[...] = products
+    send_b[...] = fold(jnp.where(step >= switch[0], by_new, by_old))
     to_group(send_b, recv_b, 1, -1, True)
-    recv_b[0] = products[0]
+    recv_b[0] = send_b[0]
     part_1 = stale(1)
 
     whole(recv_b.at[rest], recv_sem.at[1]).wait()
-    attended_0 = merge(jnp.sum(recv_b[...], axis=0) * scale_0, part_0)
+    summed = jnp.sum(recv_b[...].astype(F32), axis=0)
+    attended_0 = merge(summed[:ROWS] * scale_0, summed[ROWS:] * scale_0, part_0)
     own = stack_rows(own_v[...])
     hidden = [own[:, i * HD : (i + 1) * HD] + attended_0[i] for i in range(QPK)]
     for h in range(2):
@@ -356,7 +359,7 @@
     whole(new_1, recv_sem.at[4]).wait()
     whole(recv_c, recv_sem.at[2]).wait()
     flat = flatten(recv_c[...].astype(F32))
-    send_d[...] = jnp.dot(flat, new_1[...], preferred_element_type=F32).reshape(groups, ROWS, -1)
+    send_d[...] = fold(jnp.dot(flat, new_1[...], preferred_element_type=F32))
     for k in range(groups):
         peer = lax.rem(g + k, groups)
         put(send_d.at[peer], recv_d.at[2 * t + core], device(peer, column), 3)
@@ -367,11 +370,13 @@
     wide = jnp.concatenate([part[at : at + ROWS] for part in parts for at in (0, ROWS)], axis=1)
     scale_1 = lax.rsqrt(jnp.sum(wide * wide, axis=1, keepdims=True) / width + 1e-05)
     by_old = jnp.dot(wide.astype(BF16), old_1[...], preferred_element_type=F32)
-    row_step = lax.broadcasted_iota(jnp.int32, by_old.shape, 0) // SEQS
+    use_new = lax.broadcasted_iota(jnp.int32, (ROWS, HD), 0) // SEQS >= switch[1]
 
     whole(recv_d, recv_sem.at[3]).wait()
-    summed = jnp.where(row_step >= switch[1], jnp.sum(recv_d[...], axis=0), by_old)
-    attended_1 = merge(summed * scale_1, part_1)
+    summed = jnp.sum(recv_d[...].astype(F32), axis=0)
+    key = jnp.where(use_new, summed[:ROWS], by_old[:, :HD]) * scale_1
+    value = jnp.where(use_new, summed[ROWS:], by_old[:, HD:]) * scale_1
+    attended_1 = merge(key, value, part_1)
     for i in range(QPK):
         rows = (hidden[i] + attended_1[i]).astype(BF16)
         out[0, :, i * HD : (i + 1) * HD] = rows[:SEQS]
@@ -397,7 +402,8 @@
 def solution(mesh):
     groups, tensors = mesh.shape["group"], mesh.shape["tensor"]
 
-    def per_device(tokens, queries, cache_kv, old_kv, new_kv, switch, lengths):
+    def per_device(*operands):
+        tokens, queries, cache_kv, old_kv, new_kv, switch, lengths = operands
         depth = new_kv.shape[1]
         half = depth // 2
         block = tokens.shape[2] // tensors
@@ -423,13 +429,13 @@
                 vmem((depth, 2 * HD), BF16),
                 vmem((groups, 2 * ROWS, half), BF16),
                 vmem((groups, 2 * ROWS, half), BF16),
-                vmem((groups, ROWS, 2 * HD), F32),
-                vmem((groups, ROWS, 2 * HD), F32),
+                vmem((groups, 2 * ROWS, HD), BF16),
+                vmem((groups, 2 * ROWS, HD), BF16),
                 vmem((2, 2 * ROWS, half), BF16),
                 vmem((groups, 2 * ROWS, half), BF16),
                 vmem((tensors, 2, 2 * ROWS, half), BF16),
-                vmem((groups, ROWS, 2 * HD), F32),
-                vmem((groups, ROWS, 2 * HD), F32),
+                vmem((groups, 2 * ROWS, HD), BF16),
+                vmem((groups, 2 * ROWS, HD), BF16),
                 pltpu.SemaphoreType.DMA((8,)),
                 pltpu.SemaphoreType.DMA((LAYERS, 2)),
                 pltpu.SemaphoreType.DMA((LAYERS, 2)),
@@ -439,9 +445,9 @@
                 pltpu.SemaphoreType.REGULAR,
             ],
             compiler_params=pltpu.CompilerParams(
-                collective_id=0, has_side_effects=True, vmem_limit_bytes=56 * 2**20
+                collective_id=0, has_side_effects=True, vmem_limit_bytes=40 * 2**20
             ),
-        )(tokens, queries, cache_kv, old_kv, new_kv, switch, lengths)
+        )(*[pltpu.with_memory_space_constraint(operand, pltpu.HBM) for operand in operands])
         return result
 
     return jax.shard_map(

time: 32 us -> 29.9 us (0.934)
  Pallas kernels: 30.5 us -> 29.1 us
  local copies, waits for them, and re-layouts: 1.33 us -> 0.61 us
    pallas_call x1, Pallas kernels: 30.5 us -> 29.1 us  [per_device(): pl.pallas_call(functools.partial(kernel, groups, tensors), out_shape=jax....]
    unnamed x1, local copies, waits for them, and re-layouts: 1.33 us -> 0.61 us
where the time goes in v4:
time: 29.9 us; the launch traced here: 29.8 us
  Pallas kernels  29.1 us (97%)
  local copies, waits for them, and re-layouts  0.61 us (2%)
    pallas_call x1, Pallas kernels, per_device(): pl.pallas_call(functools.partial(kernel, groups, tensors), out_shape=jax....  29.1 us
    unnamed x1, local copies, waits for them, and re-layouts  0.61 us

profile of v4, /device:TPU:1, one launch (start us, length us, event | category | flops | bytes accessed | tf_op | source)
XLA Modules:
  0.0 29.8 jit_solution(9017415299092762999)
XLA Ops:
  0.0 29.1 %shard_map.73 = bf16[2,4,1024]{2,1,0:T(4,128)(2,1)S(1)} custom-call(bf16[2,4,8192]{2,1,0:T(4,128)(2,1)} %tokens.1, bf16[2,2,4,1024]{3,2,1,0:T(4,128)(2,1)} %queries.1, bf16[2,4,2048,256]{3,2,1,0:T(8,128)(2,1)} %cache.1, bf16[2,8192,256]{2,1,0:T(8,128)(2,1)} %old_kv.1, bf16[2,512,256]{2,1,0:T(8,128)(2,1)} %new_kv.1, s32[2]{0:T(128)} %switch_hbm.1, s32[4]{0:T(128)} %lengths_hbm.1), custom_call_target="tpu_custom_call" | custom-call | tf_op jit(solution)/shard_map/pallas_call | solution.py:413
  29.2 0.6 %copy.9 = bf16[2,4,1024]{2,1,0:T(4,128)(2,1)} copy(bf16[2,4,1024]{2,1,0:T(4,128)(2,1)S(1)} %shard_map.73) | data formatting | bytes 32768

commit v5 on v4

--- a/solution.py
+++ b/solution.py
@@ -77,14 +77,14 @@
         return {"group": group, "tensor": tensor}
 
     def holder(row_block, column_block):
-        side = lax.rem(row_block, 2)
-        across = lax.rem(row_block // 4 + column_block // 2 + 2 * side, 4)
-        along = lax.rem(row_block // 2 + column_block + side, 2)
-        return 4 * across + 2 * along + side
+        across = lax.rem(row_block // 4 + column_block + 1, 4)
+        along = lax.rem(row_block // 2 + column_block // 4 + column_block, 2)
+        return 4 * across + 2 * along + lax.rem(row_block, 2)
 
     def route(side):
         goes = device(holder(2 * (g // 2) + side, t), g // 2)
-        return goes, 2 * lax.rem(x + 8 - t // 2 - 2 * side, 4) + lax.rem(y + t + side, 2)
+        low = lax.rem(x + 7 - t // 2, 4)
+        return goes, 4 * lax.rem(y + t + low, 2) + low
 
     def targets(side):
         goes, columns = route(side)
@@ -167,11 +167,6 @@
     ]
     for copy in loads:
         copy.start()
-    for layer in range(LAYERS):
-        for j in range(2):
-            longs[layer][j].start()
-            shorts[layer][j].start()
-    late.start()
 
     loads[0].wait()
     mine = stack_rows(tok_v[...])
@@ -207,9 +202,23 @@
     def whole(ref, sem):
         return pltpu.make_async_copy(ref, ref, sem)
 
+    steps = [
+        (along_x, along_y, along_core)
+        for along_x, along_y in ((2, 1), (2, 0), (1, 1), (3, 1), (1, 0), (3, 0), (0, 1), (0, 0))
+        for along_core in (1, 0)
+    ][:-1]
+
+    def step_from(sign, step):
+        along_x, along_y, along_core = step
+        return (
+            4 * lax.rem(x + 4 + sign * along_x, 4)
+            + 2 * lax.rem(y + along_y, 2)
+            + lax.rem(core + along_core, 2)
+        )
+
     def to_group(src, dst, phase, sign, by_slot):
-        for k in range(1, groups):
-            peer = lax.rem(g + (groups + sign * k), groups)
+        for k, step in enumerate(steps, 1):
+            peer = step_from(sign, step)
             pltpu.make_async_remote_copy(
                 src_ref=src.at[k if by_slot else peer],
                 dst_ref=dst.at[k],
@@ -238,8 +247,13 @@
         def _():
             pltpu.make_async_copy(src, dst, recv_sem.at[phase]).start()
 
+    for layer in range(LAYERS):
+        for j in range(2):
+            longs[layer][j].start()
+            shorts[layer][j].start()
+    late.start()
     far_barrier()
-    put(new_kv.at[1], new_1, there, 4)
+    put(new_kv.at[1, pl.ds(0,320)], new_1.at[pl.ds(0,320)], there, 4)
 
     row = lax.broadcasted_iota(jnp.int32, (QPK * ROWS, 1), 0)
     row_seq = lax.rem(row, SEQS)
@@ -317,16 +331,17 @@
     flat = flatten(recv_a[...].astype(F32))
     by_new = jnp.dot(flat, new_0[...], preferred_element_type=F32)
     by_old = jnp.dot(flat, old_0[...], preferred_element_type=F32)
-    step = lax.rem(lax.broadcasted_iota(jnp.int32, by_new.shape, 0), ROWS) // SEQS
-    send_b[...] = fold(jnp.where(step >= switch[0], by_new, by_old))
+    row_step = lax.rem(lax.broadcasted_iota(jnp.int32, by_new.shape, 0), ROWS) // SEQS
+    send_b[...] = fold(jnp.where(row_step >= switch[0], by_new, by_old))
     to_group(send_b, recv_b, 1, -1, True)
+    put(new_kv.at[1, pl.ds(320,192)], new_1.at[pl.ds(320,192)], there, 4)
     recv_b[0] = send_b[0]
     part_1 = stale(1)
 
+    own = stack_rows(own_v[...])
     whole(recv_b.at[rest], recv_sem.at[1]).wait()
     summed = jnp.sum(recv_b[...].astype(F32), axis=0)
     attended_0 = merge(summed[:ROWS] * scale_0, summed[ROWS:] * scale_0, part_0)
-    own = stack_rows(own_v[...])
     hidden = [own[:, i * HD : (i + 1) * HD] + attended_0[i] for i in range(QPK)]
     for h in range(2):
         send_c[h] = jnp.concatenate(
@@ -334,10 +349,10 @@
             axis=0,
         ).astype(BF16)
 
-    for k in range(1, groups):
-        peer = lax.rem(g + k, groups)
+    for step in steps:
+        peer = step_from(1, step)
         pltpu.make_async_remote_copy(
-            src_ref=send_c.at[lax.rem(peer, 2)],
+            src_ref=send_c.at[lax.rem(core + step[2], 2)],
             dst_ref=recv_c.at[g],
             send_sem=send_sem.at[2],
             recv_sem=recv_sem.at[2],
@@ -360,8 +375,7 @@
     whole(recv_c, recv_sem.at[2]).wait()
     flat = flatten(recv_c[...].astype(F32))
     send_d[...] = fold(jnp.dot(flat, new_1[...], preferred_element_type=F32))
-    for k in range(groups):
-        peer = lax.rem(g + k, groups)
+    for peer in (1, 0, 3, 2, 13, 12, 5, 4, 15, 14, 7, 6, 9, 8, 11, 10):
         put(send_d.at[peer], recv_d.at[2 * t + core], device(peer, column), 3)
 
     late.wait()

time: 29.9 us -> 27.7 us (0.926)
  Pallas kernels: 29.1 us -> 26.9 us
    pallas_call x1, Pallas kernels: 29.1 us -> 26.9 us  [per_device(): pl.pallas_call(functools.partial(kernel, groups, tensors), out_shape=jax....]
where the time goes in v5:
time: 27.7 us; the launch traced here: 27.5 us
  Pallas kernels  26.9 us (97%)
  local copies, waits for them, and re-layouts  0.61 us (2%)
    pallas_call x1, Pallas kernels, per_device(): pl.pallas_call(functools.partial(kernel, groups, tensors), out_shape=jax....  26.9 us
    unnamed x1, local copies, waits for them, and re-layouts  0.61 us

profile of v5, /device:TPU:1, one launch (start us, length us, event | category | flops | bytes accessed | tf_op | source)
XLA Modules:
  0.0 27.5 jit_solution(4589090982260011813)
XLA Ops:
  0.0 26.9 %shard_map.73 = bf16[2,4,1024]{2,1,0:T(4,128)(2,1)S(1)} custom-call(bf16[2,4,8192]{2,1,0:T(4,128)(2,1)} %tokens.1, bf16[2,2,4,1024]{3,2,1,0:T(4,128)(2,1)} %queries.1, bf16[2,4,2048,256]{3,2,1,0:T(8,128)(2,1)} %cache.1, bf16[2,8192,256]{2,1,0:T(8,128)(2,1)} %old_kv.1, bf16[2,512,256]{2,1,0:T(8,128)(2,1)} %new_kv.1, s32[2]{0:T(128)} %switch_hbm.1, s32[4]{0:T(128)} %lengths_hbm.1), custom_call_target="tpu_custom_call" | custom-call | tf_op jit(solution)/shard_map/pallas_call | solution.py:427
  26.9 0.6 %copy.9 = bf16[2,4,1024]{2,1,0:T(4,128)(2,1)} copy(bf16[2,4,1024]{2,1,0:T(4,128)(2,1)S(1)} %shard_map.73) | data formatting | bytes 32768

commit v6 on v5

--- a/solution.py
+++ b/solution.py
@@ -119,6 +119,9 @@
     def _():
         greet(mate)
 
+    load_tokens = pltpu.make_async_copy(tokens, tok_v, load_sem.at[0])
+    load_tokens.start()
+
     for k in range(1, tensors):
         greet(device(g - core + 1, lax.rem(t + k, tensors)))
     for other in senders():
@@ -128,7 +131,7 @@
             greet(device(2 * (other["group"] // 2) + 1, other["tensor"]))
 
     loads = [
-        pltpu.make_async_copy(tokens, tok_v, load_sem.at[0]),
+        load_tokens,
         pltpu.make_async_copy(
             tokens.at[:, :, pl.ds(pl.multiple_of(t * block, block), block)],
             own_v,
@@ -165,7 +168,7 @@
         ]
         for layer in range(LAYERS)
     ]
-    for copy in loads:
+    for copy in loads[1:]:
         copy.start()
 
     loads[0].wait()
@@ -253,7 +256,7 @@
             shorts[layer][j].start()
     late.start()
     far_barrier()
-    put(new_kv.at[1, pl.ds(0,320)], new_1.at[pl.ds(0,320)], there, 4)
+    put(new_kv.at[1, pl.ds(0,256)], new_1.at[pl.ds(0,256)], there, 4)
 
     row = lax.broadcasted_iota(jnp.int32, (QPK * ROWS, 1), 0)
     row_seq = lax.rem(row, SEQS)
@@ -324,7 +327,6 @@
 
     for copy in loads[1:]:
         copy.wait()
-    part_0 = stale(0)
 
     rest = pl.ds(1, groups - 1)
     whole(recv_a.at[rest], recv_sem.at[0]).wait()
@@ -334,9 +336,9 @@
     row_step = lax.rem(lax.broadcasted_iota(jnp.int32, by_new.shape, 0), ROWS) // SEQS
     send_b[...] = fold(jnp.where(row_step >= switch[0], by_new, by_old))
     to_group(send_b, recv_b, 1, -1, True)
-    put(new_kv.at[1, pl.ds(320,192)], new_1.at[pl.ds(320,192)], there, 4)
+    put(new_kv.at[1, pl.ds(256,256)], new_1.at[pl.ds(256,256)], there, 4)
     recv_b[0] = send_b[0]
-    part_1 = stale(1)
+    part_0 = stale(0)
 
     own = stack_rows(own_v[...])
     whole(recv_b.at[rest], recv_sem.at[1]).wait()
@@ -371,6 +373,7 @@
         ).start()
     pltpu.make_async_copy(send_c, recv_t.at[t], recv_sem.at[5]).start()
 
+    part_1 = stale(1)
     whole(new_1, recv_sem.at[4]).wait()
     whole(recv_c, recv_sem.at[2]).wait()
     flat = flatten(recv_c[...].astype(F32))

time: 27.7 us -> 27.2 us (0.982)
  Pallas kernels: 26.9 us -> 26.5 us
    pallas_call x1, Pallas kernels: 26.9 us -> 26.5 us  [per_device(): pl.pallas_call(functools.partial(kernel, groups, tensors), out_shape=jax....]
where the time goes in v6:
time: 27.2 us; the launch traced here: 27.1 us
  Pallas kernels  26.5 us (97%)
  local copies, waits for them, and re-layouts  0.61 us (2%)
    pallas_call x1, Pallas kernels, per_device(): pl.pallas_call(functools.partial(kernel, groups, tensors), out_shape=jax....  26.5 us
    unnamed x1, local copies, waits for them, and re-layouts  0.61 us

profile of v6, /device:TPU:1, one launch (start us, length us, event | category | flops | bytes accessed | tf_op | source)
XLA Modules:
  0.0 27.1 jit_solution(5517736230105512989)
XLA Ops:
  0.0 26.5 %shard_map.73 = bf16[2,4,1024]{2,1,0:T(4,128)(2,1)S(1)} custom-call(bf16[2,4,8192]{2,1,0:T(4,128)(2,1)} %tokens.1, bf16[2,2,4,1024]{3,2,1,0:T(4,128)(2,1)} %queries.1, bf16[2,4,2048,256]{3,2,1,0:T(8,128)(2,1)} %cache.1, bf16[2,8192,256]{2,1,0:T(8,128)(2,1)} %old_kv.1, bf16[2,512,256]{2,1,0:T(8,128)(2,1)} %new_kv.1, s32[2]{0:T(128)} %switch_hbm.1, s32[4]{0:T(128)} %lengths_hbm.1), custom_call_target="tpu_custom_call" | custom-call | tf_op jit(solution)/shard_map/pallas_call | solution.py:430
  26.5 0.6 %copy.9 = bf16[2,4,1024]{2,1,0:T(4,128)(2,1)} copy(bf16[2,4,1024]{2,1,0:T(4,128)(2,1)S(1)} %shard_map.73) | data formatting | bytes 32768

commit v7 on v6

--- a/solution.py
+++ b/solution.py
@@ -207,7 +207,7 @@
 
     steps = [
         (along_x, along_y, along_core)
-        for along_x, along_y in ((2, 1), (2, 0), (1, 1), (3, 1), (1, 0), (3, 0), (0, 1), (0, 0))
+        for along_x, along_y in ((2, 1), (1, 1), (3, 1), (2, 0), (1, 0), (3, 0), (0, 1), (0, 0))
         for along_core in (1, 0)
     ][:-1]
 
@@ -255,8 +255,12 @@
             longs[layer][j].start()
             shorts[layer][j].start()
     late.start()
+    def move(piece):
+        rows = pl.ds(piece * (depth // 4), depth // 4)
+        put(new_kv.at[1, rows], new_1.at[rows], there, 4)
+
     far_barrier()
-    put(new_kv.at[1, pl.ds(0,256)], new_1.at[pl.ds(0,256)], there, 4)
+    move(0)
 
     row = lax.broadcasted_iota(jnp.int32, (QPK * ROWS, 1), 0)
     row_seq = lax.rem(row, SEQS)
@@ -329,6 +333,8 @@
         copy.wait()
 
     rest = pl.ds(1, groups - 1)
+    part_0 = stale(0)
+    move(1)
     whole(recv_a.at[rest], recv_sem.at[0]).wait()
     flat = flatten(recv_a[...].astype(F32))
     by_new = jnp.dot(flat, new_0[...], preferred_element_type=F32)
@@ -336,9 +342,10 @@
     row_step = lax.rem(lax.broadcasted_iota(jnp.int32, by_new.shape, 0), ROWS) // SEQS
     send_b[...] = fold(jnp.where(row_step >= switch[0], by_new, by_old))
     to_group(send_b, recv_b, 1, -1, True)
-    put(new_kv.at[1, pl.ds(256,256)], new_1.at[pl.ds(256,256)], there, 4)
+    move(2)
+    part_1 = stale(1)
+    move(3)
     recv_b[0] = send_b[0]
-    part_0 = stale(0)
 
     own = stack_rows(own_v[...])
     whole(recv_b.at[rest], recv_sem.at[1]).wait()
@@ -373,7 +380,6 @@
         ).start()
     pltpu.make_async_copy(send_c, recv_t.at[t], recv_sem.at[5]).start()
 
-    part_1 = stale(1)
     whole(new_1, recv_sem.at[4]).wait()
     whole(recv_c, recv_sem.at[2]).wait()
     flat = flatten(recv_c[...].astype(F32))

time: 27.2 us -> 26.9 us (0.989)
  Pallas kernels: 26.5 us -> 26.1 us
    pallas_call x1, Pallas kernels: 26.5 us -> 26.1 us  [per_device(): pl.pallas_call(functools.partial(kernel, groups, tensors), out_shape=jax....]
where the time goes in v7:
time: 26.9 us; the launch traced here: 26.7 us
  Pallas kernels  26.1 us (97%)
  local copies, waits for them, and re-layouts  0.61 us (2%)
    pallas_call x1, Pallas kernels, per_device(): pl.pallas_call(functools.partial(kernel, groups, tensors), out_shape=jax....  26.1 us
    unnamed x1, local copies, waits for them, and re-layouts  0.61 us

profile of v7, /device:TPU:1, one launch (start us, length us, event | category | flops | bytes accessed | tf_op | source)
XLA Modules:
  0.0 26.7 jit_solution(16686771017617698107)
XLA Ops:
  0.0 26.1 %shard_map.73 = bf16[2,4,1024]{2,1,0:T(4,128)(2,1)S(1)} custom-call(bf16[2,4,8192]{2,1,0:T(4,128)(2,1)} %tokens.1, bf16[2,2,4,1024]{3,2,1,0:T(4,128)(2,1)} %queries.1, bf16[2,4,2048,256]{3,2,1,0:T(8,128)(2,1)} %cache.1, bf16[2,8192,256]{2,1,0:T(8,128)(2,1)} %old_kv.1, bf16[2,512,256]{2,1,0:T(8,128)(2,1)} %new_kv.1, s32[2]{0:T(128)} %switch_hbm.1, s32[4]{0:T(128)} %lengths_hbm.1), custom_call_target="tpu_custom_call" | custom-call | tf_op jit(solution)/shard_map/pallas_call | solution.py:436
  26.1 0.6 %copy.9 = bf16[2,4,1024]{2,1,0:T(4,128)(2,1)} copy(bf16[2,4,1024]{2,1,0:T(4,128)(2,1)S(1)} %shard_map.73) | data formatting | bytes 32768

commit v8 on v7

--- a/solution.py
+++ b/solution.py
@@ -208,8 +208,9 @@
     steps = [
         (along_x, along_y, along_core)
         for along_x, along_y in ((2, 1), (1, 1), (3, 1), (2, 0), (1, 0), (3, 0), (0, 1), (0, 0))
-        for along_core in (1, 0)
-    ][:-1]
+        for along_core in (0, 1)
+        if along_x or along_y or along_core
+    ]
 
     def step_from(sign, step):
         along_x, along_y, along_core = step

time: 26.9 us -> 26.7 us (level)
  no operation moved by 1% of the time
where the time goes in v8:
time: 26.7 us; the launch traced here: 26.6 us
  Pallas kernels  26 us (97%)
  local copies, waits for them, and re-layouts  0.61 us (2%)
    pallas_call x1, Pallas kernels, per_device(): pl.pallas_call(functools.partial(kernel, groups, tensors), out_shape=jax....  26 us
    unnamed x1, local copies, waits for them, and re-layouts  0.61 us

profile of v8, /device:TPU:1, one launch (start us, length us, event | category | flops | bytes accessed | tf_op | source)
XLA Modules:
  0.0 26.6 jit_solution(16624383656072640042)
XLA Ops:
  0.0 26.0 %shard_map.73 = bf16[2,4,1024]{2,1,0:T(4,128)(2,1)S(1)} custom-call(bf16[2,4,8192]{2,1,0:T(4,128)(2,1)} %tokens.1, bf16[2,2,4,1024]{3,2,1,0:T(4,128)(2,1)} %queries.1, bf16[2,4,2048,256]{3,2,1,0:T(8,128)(2,1)} %cache.1, bf16[2,8192,256]{2,1,0:T(8,128)(2,1)} %old_kv.1, bf16[2,512,256]{2,1,0:T(8,128)(2,1)} %new_kv.1, s32[2]{0:T(128)} %switch_hbm.1, s32[4]{0:T(128)} %lengths_hbm.1), custom_call_target="tpu_custom_call" | custom-call | tf_op jit(solution)/shard_map/pallas_call | solution.py:437
  26.0 0.6 %copy.9 = bf16[2,4,1024]{2,1,0:T(4,128)(2,1)} copy(bf16[2,4,1024]{2,1,0:T(4,128)(2,1)S(1)} %shard_map.73) | data formatting | bytes 32768
